TPU v7x, 512 devices: a whole 4x4x16 slice. The times are simulated.
512 devices in a mesh: dp: 256 (over x, z, y_hi, core), pair: 2 (over y_lo).
Axes of the slice: x: 4, y: 4 (y_hi: 2, y_lo: 2; y = y_hi * 2 + y_lo), z: 16, core: 2. Of those that a mesh axis runs over, the one named last changes fastest.
Arguments:
- picture_features: float32 [131072, 1152], P(('dp', 'pair')), may hold values from -0.18 to 0.18
- caption_features: float32 [131072, 1152], P('dp'), may hold values from -0.18 to 0.18
- sharpness_factor: float32 [1], replicated, may hold values from 20 to 40
- score_intercept: float32 [1], replicated, may hold values from -4 to -1
Outputs:
- image_grad: float32 [131072, 1152], P(('dp', 'pair'))
- text_grad: float32 [131072, 1152], P(('dp', 'pair'))
All inputs are finite; a program needn't handle non-finite values.
Results may differ from a plain program's by a relative error of at most 0.0003.
Values sent between devices are 32-bit elements; how exact they have to be, the bound alone decides.
A program may use at most 64 MiB of HBM per device.

v0:
```python
import jax
import jax.numpy as jnp
from jax import lax
from jax.sharding import PartitionSpec as P

WINDOW = 4


def passed_along(value, axis, steps):
    count = lax.axis_size(axis)
    pairs = [(source, (source + steps) % count) for source in range(count)]
    return lax.ppermute(value, axis, pairs)


def score_block(
    image_rows, text_rows, similarity_multiplier, diagonal_displacement, first, rotate_text_rows
):
    high = lax.Precision.HIGHEST
    similarity_matrix = (
        similarity_multiplier * jnp.dot(image_rows, text_rows.T, precision=high)
        + diagonal_displacement
    )
    if first:
        row_numbers = lax.broadcasted_iota(jnp.int32, similarity_matrix.shape, 0) + rotate_text_rows
        col_ids = lax.broadcasted_iota(jnp.int32, similarity_matrix.shape, 1)
        sign = jnp.where(row_numbers == col_ids, 1.0, -1.0).astype(jnp.float32)
    else:
        sign = -jnp.ones(similarity_matrix.shape, jnp.float32)
    coef = -sign * jax.nn.sigmoid(-sign * similarity_matrix)
    image_part = similarity_multiplier * jnp.dot(coef, text_rows, precision=high)
    text_portion = similarity_multiplier * jnp.dot(coef.T, image_rows, precision=high)
    return (image_part, text_portion)


def shards(picture_features, caption_features, sharpness_factor, score_intercept):
    similarity_multiplier = sharpness_factor[0]
    diagonal_displacement = score_intercept[0]
    midpoint_entries = picture_features.shape[0]
    rotate_text_rows = lax.axis_index("pair") * midpoint_entries
    text_rows = caption_features
    text_accumulator = jnp.zeros(caption_features.shape, jnp.float32)
    image_acc = jnp.zeros(picture_features.shape, jnp.float32)
    for step in range(WINDOW):
        if step > 0:
            text_rows = passed_along(text_rows, "dp", 1)
            text_accumulator = passed_along(text_accumulator, "dp", 1)
        image_part, text_portion = score_block(
            picture_features,
            text_rows,
            similarity_multiplier,
            diagonal_displacement,
            step == 0,
            rotate_text_rows,
        )
        image_acc = image_acc + image_part
        text_accumulator = text_accumulator + text_portion
    text_accumulator = passed_along(text_accumulator, "dp", 1 - WINDOW)
    text_grad = lax.psum_scatter(text_accumulator, "pair", scatter_dimension=0, tiled=True)
    return (image_acc, text_grad)


def solution(mesh):
    return jax.shard_map(
        shards,
        mesh=mesh,
        in_specs=(P(("dp", "pair"), None), P("dp", None), P(), P()),
        out_specs=(P(("dp", "pair"), None), P(("dp", "pair"), None)),
        check_vma=False,
    )
```

profile of v0, /device:TPU:1, one launch (start us, length us, event | category | flops | bytes accessed | tf_op | source)
XLA Modules:
  0.0 279.7 jit_solution(10878689926387404508)
XLA Ops:
  7.2 0.0 copy-start
  7.2 0.0 reduce-scatter.2.cloned.1.call-start
  7.2 6.3 %collective-permute-start = (f32[512,1152]{1,0:T(8,128)}, f32[512,1152]{1,0:T(8,128)S(1)}, u32[]{:S(2)}, u32[]{:S(2)}) collective-permute-start(f32[512,1152]{1,0:T(8,128)} %param.5), channel_id=1, source_target_pairs={{0,2},{2,4},{4,6},{6,8},{8,10},{10,12},{12,14},{14,16},{16,18},{18... | collective-permute-start | bytes 7077896 | tf_op jit(solution)/shard_map/ppermute | solution.py:12
  14.9 0.0 copy-done
  14.9 4.2 %fusion.23 = f32[256,512]{1,0:T(8,128)S(1)} fusion(f32[256,1152]{1,0:T(8,128)S(1)} %copy-done, f32[512,1152]{1,0:T(8,128)} %param.5, f32[]{:T(128)} %bitcast.35, f32[]{:T(128)} %bitcast.27, s32[256]{0:T(256)S(1)} %iota_add_fusion), kind=kOutput, calls=%fused_computation.34 | convolution fusion | flops 1813250048 | bytes 4064264 | tf_op jit(solution)/shard_map/dot_general | solution.py:20
  19.0 0.0 copy-start.11
  19.1 2.5 convolution_multiply_fusion.3
  21.5 1.9 collective-permute-start.3
  23.5 16.2 %collective-permute-done = f32[512,1152]{1,0:T(8,128)S(1)} collective-permute-done((f32[512,1152]{1,0:T(8,128)}, f32[512,1152]{1,0:T(8,128)S(1)}, u32[]{:S(2)}, u32[]{:S(2)}) %collective-permute-start) | collective-permute-done | bytes 2359328 | tf_op jit(solution)/shard_map/ppermute | solution.py:12
  39.7 5.8 %collective-permute-start.1 = (f32[512,1152]{1,0:T(8,128)S(1)}, f32[512,1152]{1,0:T(8,128)S(1)}, u32[]{:S(2)}, u32[]{:S(2)}) collective-permute-start(f32[512,1152]{1,0:T(8,128)S(1)} %collective-permute-done), channel_id=1, source_target_pairs={{0,2},{2,4},{4,6},{6,8},{8,10},{10,12},{12,14},{14,16},{16,18},{18... | collective-permute-start | bytes 7077896 | tf_op jit(solution)/shard_map/ppermute | solution.py:12
  45.4 2.4 fusion.17
  47.9 0.0 copy-start.5
  47.9 17.0 %collective-permute-done.3 = f32[512,1152]{1,0:T(8,128)S(1)} collective-permute-done((f32[512,1152]{1,0:T(8,128)S(1)}, f32[512,1152]{1,0:T(8,128)S(1)}, u32[]{:S(2)}, u32[]{:S(2)}) %collective-permute-start.3) | collective-permute-done | bytes 2359328 | tf_op jit(solution)/shard_map/ppermute | solution.py:12
  64.8 0.0 copy-done.11
  64.8 2.6 fusion
  67.4 0.0 copy-done.5
  67.4 5.9 %collective-permute-start.4 = (f32[512,1152]{1,0:T(8,128)S(1)}, f32[512,1152]{1,0:T(8,128)S(1)}, u32[]{:S(2)}, u32[]{:S(2)}) collective-permute-start(f32[512,1152]{1,0:T(8,128)S(1)} %fusion), channel_id=1, source_target_pairs={{0,2},{2,4},{4,6},{6,8},{8,10},{10,12},{12,14},{14,16},{16,18},{18... | collective-permute-start | bytes 7077896 | tf_op jit(solution)/shard_map/ppermute | solution.py:12
  73.3 16.8 %collective-permute-done.1 = f32[512,1152]{1,0:T(8,128)S(1)} collective-permute-done((f32[512,1152]{1,0:T(8,128)S(1)}, f32[512,1152]{1,0:T(8,128)S(1)}, u32[]{:S(2)}, u32[]{:S(2)}) %collective-permute-start.1) | collective-permute-done | bytes 2359328 | tf_op jit(solution)/shard_map/ppermute | solution.py:12
  90.1 0.0 copy-start.1
  90.1 6.1 %collective-permute-start.2 = (f32[512,1152]{1,0:T(8,128)S(1)}, f32[512,1152]{1,0:T(8,128)S(1)}, u32[]{:S(2)}, u32[]{:S(2)}) collective-permute-start(f32[512,1152]{1,0:T(8,128)S(1)} %collective-permute-done.1), channel_id=1, source_target_pairs={{0,2},{2,4},{4,6},{6,8},{8,10},{10,12},{12,14},{14,16},{16,18},{18... | collective-permute-start | bytes 7077896 | tf_op jit(solution)/shard_map/ppermute | solution.py:12
  96.2 2.4 fusion.15
  98.6 0.0 copy-start.7
  98.6 0.8 copy-done.7
  99.4 2.5 convolution_multiply_fusion.1
  101.9 0.0 copy-done.1
  101.9 13.5 %collective-permute-done.4 = f32[512,1152]{1,0:T(8,128)S(1)} collective-permute-done((f32[512,1152]{1,0:T(8,128)S(1)}, f32[512,1152]{1,0:T(8,128)S(1)}, u32[]{:S(2)}, u32[]{:S(2)}) %collective-permute-start.4) | collective-permute-done | bytes 2359328 | tf_op jit(solution)/shard_map/ppermute | solution.py:12
  115.4 0.2 add.72
  115.6 5.9 %collective-permute-start.5 = (f32[512,1152]{1,0:T(8,128)S(1)}, f32[512,1152]{1,0:T(8,128)S(1)}, u32[]{:S(2)}, u32[]{:S(2)}) collective-permute-start(f32[512,1152]{1,0:T(8,128)S(1)} %add.72), channel_id=1, source_target_pairs={{0,2},{2,4},{4,6},{6,8},{8,10},{10,12},{12,14},{14,16},{16,18},{18... | collective-permute-start | bytes 7077896 | tf_op jit(solution)/shard_map/ppermute | solution.py:12
  121.5 19.1 %collective-permute-done.2 = f32[512,1152]{1,0:T(8,128)S(1)} collective-permute-done((f32[512,1152]{1,0:T(8,128)S(1)}, f32[512,1152]{1,0:T(8,128)S(1)}, u32[]{:S(2)}, u32[]{:S(2)}) %collective-permute-start.2) | collective-permute-done | bytes 2359328 | tf_op jit(solution)/shard_map/ppermute | solution.py:12
  140.7 0.0 copy-start.3
  140.7 2.4 fusion.13
  143.1 0.0 copy-start.9
  143.1 2.5 convolution_multiply_fusion
  145.6 0.0 copy-done.3
  145.6 20.4 %collective-permute-done.5 = f32[512,1152]{1,0:T(8,128)S(1)} collective-permute-done((f32[512,1152]{1,0:T(8,128)S(1)}, f32[512,1152]{1,0:T(8,128)S(1)}, u32[]{:S(2)}, u32[]{:S(2)}) %collective-permute-start.5) | collective-permute-done | bytes 2359328 | tf_op jit(solution)/shard_map/ppermute | solution.py:12
  166.0 0.2 add.73
  166.2 0.0 copy-done.9
  166.2 17.2 %collective-permute-start.6 = (f32[512,1152]{1,0:T(8,128)S(1)}, f32[512,1152]{1,0:T(8,128)}, u32[]{:S(2)}, u32[]{:S(2)}) collective-permute-start(f32[512,1152]{1,0:T(8,128)S(1)} %add.73), channel_id=1, source_target_pairs={{0,506},{2,508},{4,510},{6,0},{8,2},{10,4},{12,6},{14,8},{16,10},{... | collective-permute-start | bytes 7077896 | tf_op jit(solution)/shard_map/ppermute | solution.py:12
  183.5 47.7 %collective-permute-done.6 = f32[512,1152]{1,0:T(8,128)} collective-permute-done((f32[512,1152]{1,0:T(8,128)S(1)}, f32[512,1152]{1,0:T(8,128)}, u32[]{:S(2)}, u32[]{:S(2)}) %collective-permute-start.6) | collective-permute-done | bytes 2359328 | tf_op jit(solution)/shard_map/ppermute | solution.py:12
  231.2 0.0 reduce-scatter.2.cloned.1.call-update
  231.2 0.0 copy-start.6
  231.2 4.2 %fusion.24 = f32[256,1152]{1,0:T(8,128)S(1)} fusion(f32[256,512]{1,0:T(8,128)} %copy-done.11, f32[512,1152]{1,0:T(8,128)} %param.5), kind=kOutput, calls=%fused_computation.37 | convolution fusion | flops 1811939328 | bytes 4063232 | tf_op jit(solution)/shard_map/dot_general | solution.py:30
  235.4 0.0 copy-done.6
  235.4 0.0 copy-start.2
  235.4 0.0 copy-start.8
  235.4 2.4 convolution_add_fusion.2
  237.8 0.0 copy-done.2
  237.8 0.0 copy-done.8
  237.8 0.0 copy-start.4
  237.8 0.0 copy-start.10
  237.9 2.4 convolution_add_fusion.1
  240.2 0.0 copy-done.4
  240.3 0.0 copy-done.10
  240.3 3.4 %fusion.1 = f32[256,1152]{1,0:T(8,128)} fusion(f32[256,1152]{1,0:T(8,128)S(1)} %convolution_add_fusion.1, f32[256,512]{1,0:T(8,128)S(1)} %copy-done.10, f32[512,1152]{1,0:T(8,128)S(1)} %copy-done.4, f32[]{:T(128)} %bitcast.26), kind=kOutput, calls=%fused_computation.6 | convolution fusion | flops 1812529152 | bytes 5242884 | tf_op jit(solution)/shard_map/dot_general | solution.py:30
  243.6 29.2 %reduce-scatter.2.cloned.1.call-done = f32[256,1152]{1,0:T(8,128)} async-done(((f32[512,1152]{1,0:T(8,128)}), f32[256,1152]{1,0:T(8,128)}) %reduce-scatter.2.cloned.1.call-update) | async-done | bytes 1179664 | tf_op jit(solution)/shard_map/reduce_scatter | solution.py:58
  (1 shorter events, 0.0 us)
Async XLA Ops:
  7.2 7.7 %copy-start = (f32[256,1152]{1,0:T(8,128)S(1)}, f32[256,1152]{1,0:T(8,128)}, u32[]{:S(2)}) copy-start(f32[256,1152]{1,0:T(8,128)} %param.4) | copy-start | bytes 3538948
  7.2 265.7 %reduce-scatter.2.cloned.1.call-start = ((), (), s32[]{:S(2)}) async-start(), calls=%async_computation.1 | async-start | bytes 3538944 | tf_op jit(solution)/shard_map/reduce_scatter | solution.py:58
  7.2 32.4 %collective-permute-start = (f32[512,1152]{1,0:T(8,128)}, f32[512,1152]{1,0:T(8,128)S(1)}, u32[]{:S(2)}, u32[]{:S(2)}) collective-permute-start(f32[512,1152]{1,0:T(8,128)} %param.5), channel_id=1, source_target_pairs={{0,2},{2,4},{4,6},{6,8},{8,10},{10,12},{12,14},{14,16},{16,18},{18... | collective-permute-start | bytes 7077896 | tf_op jit(solution)/shard_map/ppermute | solution.py:12
  19.0 45.8 %copy-start.11 = (f32[256,512]{1,0:T(8,128)}, f32[256,512]{1,0:T(8,128)S(1)}, u32[]{:S(2)}) copy-start(f32[256,512]{1,0:T(8,128)S(1)} %fusion.23) | copy-start | bytes 1572868
  21.5 43.3 %collective-permute-start.3 = (f32[512,1152]{1,0:T(8,128)S(1)}, f32[512,1152]{1,0:T(8,128)S(1)}, u32[]{:S(2)}, u32[]{:S(2)}) collective-permute-start(f32[512,1152]{1,0:T(8,128)S(1)} %convolution_multiply_fusion.3), channel_id=1, source_target_pairs={{0,2},{2,4},{4,6},{6,8},{8,10},{10,12},{12,14},{14,16},{16,18},{18... | collective-permute-start | bytes 7077896 | tf_op jit(solution)/shard_map/ppermute | solution.py:12
  39.7 50.5 %collective-permute-start.1 = (f32[512,1152]{1,0:T(8,128)S(1)}, f32[512,1152]{1,0:T(8,128)S(1)}, u32[]{:S(2)}, u32[]{:S(2)}) collective-permute-start(f32[512,1152]{1,0:T(8,128)S(1)} %collective-permute-done), channel_id=1, source_target_pairs={{0,2},{2,4},{4,6},{6,8},{8,10},{10,12},{12,14},{14,16},{16,18},{18... | collective-permute-start | bytes 7077896 | tf_op jit(solution)/shard_map/ppermute | solution.py:12
  47.9 19.6 %copy-start.5 = (f32[256,512]{1,0:T(8,128)}, f32[256,512]{1,0:T(8,128)S(1)}, u32[]{:S(2)}) copy-start(f32[256,512]{1,0:T(8,128)S(1)} %fusion.17) | copy-start | bytes 1572868
  67.4 48.0 %collective-permute-start.4 = (f32[512,1152]{1,0:T(8,128)S(1)}, f32[512,1152]{1,0:T(8,128)S(1)}, u32[]{:S(2)}, u32[]{:S(2)}) collective-permute-start(f32[512,1152]{1,0:T(8,128)S(1)} %fusion), channel_id=1, source_target_pairs={{0,2},{2,4},{4,6},{6,8},{8,10},{10,12},{12,14},{14,16},{16,18},{18... | collective-permute-start | bytes 7077896 | tf_op jit(solution)/shard_map/ppermute | solution.py:12
  90.1 11.8 %copy-start.1 = (f32[512,1152]{1,0:T(8,128)}, f32[512,1152]{1,0:T(8,128)S(1)}, u32[]{:S(2)}) copy-start(f32[512,1152]{1,0:T(8,128)S(1)} %collective-permute-done.1) | copy-start | bytes 7077892
  90.1 50.6 %collective-permute-start.2 = (f32[512,1152]{1,0:T(8,128)S(1)}, f32[512,1152]{1,0:T(8,128)S(1)}, u32[]{:S(2)}, u32[]{:S(2)}) collective-permute-start(f32[512,1152]{1,0:T(8,128)S(1)} %collective-permute-done.1), channel_id=1, source_target_pairs={{0,2},{2,4},{4,6},{6,8},{8,10},{10,12},{12,14},{14,16},{16,18},{18... | collective-permute-start | bytes 7077896 | tf_op jit(solution)/shard_map/ppermute | solution.py:12
  98.6 0.8 copy-start.7
  115.6 50.3 %collective-permute-start.5 = (f32[512,1152]{1,0:T(8,128)S(1)}, f32[512,1152]{1,0:T(8,128)S(1)}, u32[]{:S(2)}, u32[]{:S(2)}) collective-permute-start(f32[512,1152]{1,0:T(8,128)S(1)} %add.72), channel_id=1, source_target_pairs={{0,2},{2,4},{4,6},{6,8},{8,10},{10,12},{12,14},{14,16},{16,18},{18... | collective-permute-start | bytes 7077896 | tf_op jit(solution)/shard_map/ppermute | solution.py:12
  140.7 4.9 %copy-start.3 = (f32[512,1152]{1,0:T(8,128)}, f32[512,1152]{1,0:T(8,128)S(1)}, u32[]{:S(2)}) copy-start(f32[512,1152]{1,0:T(8,128)S(1)} %collective-permute-done.2) | copy-start | bytes 7077892
  143.1 23.1 %copy-start.9 = (f32[256,512]{1,0:T(8,128)}, f32[256,512]{1,0:T(8,128)S(1)}, u32[]{:S(2)}) copy-start(f32[256,512]{1,0:T(8,128)S(1)} %fusion.13) | copy-start | bytes 1572868
  166.2 64.9 %collective-permute-start.6 = (f32[512,1152]{1,0:T(8,128)S(1)}, f32[512,1152]{1,0:T(8,128)}, u32[]{:S(2)}, u32[]{:S(2)}) collective-permute-start(f32[512,1152]{1,0:T(8,128)S(1)} %add.73), channel_id=1, source_target_pairs={{0,506},{2,508},{4,510},{6,0},{8,2},{10,4},{12,6},{14,8},{16,10},{... | collective-permute-start | bytes 7077896 | tf_op jit(solution)/shard_map/ppermute | solution.py:12
  231.2 4.2 %copy-start.6 = (f32[256,512]{1,0:T(8,128)S(1)}, f32[256,512]{1,0:T(8,128)}, u32[]{:S(2)}) copy-start(f32[256,512]{1,0:T(8,128)} %copy-done.5) | copy-start | bytes 1572868
  235.4 2.4 copy-start.2
  235.4 2.4 copy-start.8
  237.8 2.4 copy-start.4
  237.8 2.4 copy-start.10
Sparse Core Ops, SparseCore 0:
  231.3 41.5 reduce-scatter.1
where the time goes:
time: 280 us
  waiting for transfers between devices  180 us (64%)
  starting transfers between devices  49.2 us (18%)
  matrix products  33.7 us (12%)
  between operations  15.6 us (6%)
    ppermute x7, waiting for transfers between devices, passed_along(): return lax.ppermute(value, axis, pairs)  151 us
    ppermute x7, starting transfers between devices, passed_along(): return lax.ppermute(value, axis, pairs)  49.1 us
    reduce_scatter x1, waiting for transfers between devices, shards(): lax.psum_scatter(text_accumulator, 'pair', scatter_dimension=0, tiled=True)  29.2 us
    dot_general x4, matrix products, score_block(): jnp.dot(coef, text_rows, precision=high)  12.4 us
    dot_general x4, matrix products, score_block(): jnp.dot(image_rows, text_rows.T, precision=high)  11.4 us
    dot_general x4, matrix products, score_block(): jnp.dot(coef.T, image_rows, precision=high)  9.96 us
  transfers between devices with their start and end apart: 8, of which 8 were waited for; matrix products, arithmetic and copies ran while one was open for 12% of the time, Pallas kernels for 0%

commit v1 on v0

v1 whole, which is shorter than its diff:
```python
import functools

import jax
import jax.numpy as jnp
from jax import lax
from jax.experimental import pallas as pl
from jax.experimental.pallas import tpu as pltpu
from jax.sharding import PartitionSpec as P

MESH = pl.DeviceIdType.MESH
F32, BF16 = jnp.float32, jnp.bfloat16
CHUNK = 64
OWN_CHUNK = 128


def halves(value):
    high = value.astype(BF16)
    return high, (value - high.astype(F32)).astype(BF16)


def dot(a, b):
    return jnp.dot(a, b, preferred_element_type=F32)


def kernel(
    n, scale_ref, bias_ref, pic, cap, image_out, text_out,
    img, text, t_high, t_low, tt_high, tt_low, grad, text_grad,
    part, ret, ret_far, text_ret,
    load_sem, out_sem, s1, s2, s3, sf, sp, sr, sx, st, r1, r2, r3, rp, rr, rx, rt,
):
    dp, p = lax.axis_index("dp"), lax.axis_index("pair")
    half, words = pic.shape[0], cap.shape[0]
    chunks = half // CHUNK
    core = lax.rem(dp, 2)
    low = lax.rem(dp, 4) < 2
    a0 = low & (core == 0)
    a1 = low & (core == 1)
    b0 = jnp.logical_not(low) & (core == 0)

    def there(step, row):
        return (lax.rem(dp + step + n, n), row)

    q = 1 - p
    sibling = there(1 - 2 * core, p)
    down, up = there(-2, q), there(2, q)
    across = there(jnp.where(core == 1, 1, -1), q)
    far = there(jnp.where(core == 1, 3, -3), p)
    first_to = there(jnp.where(core == 1, -1, -3), p)
    first_back = there(jnp.where(core == 1, 3, 1), p)
    partner = (dp, q)
    main, other = 2 + core, 3 - core

    def rows(k, size=CHUNK):
        return pl.ds(pl.multiple_of(k * size, size), size)

    def remote(src, dst, send, recv, device):
        return pltpu.make_async_remote_copy(
            src_ref=src, dst_ref=dst, send_sem=send, recv_sem=recv, device_id=device, device_id_type=MESH
        )

    def each(body, count=chunks):
        def run(k, _):
            body(k)
            return 0

        lax.fori_loop(0, count, run, 0)

    def send_main(k):
        return remote(pic.at[rows(k)], img.at[main, rows(k)], s2.at[k], r2.at[k], down)

    def send_first(k):
        return remote(pic.at[rows(k)], img.at[1, rows(k)], s1.at[k], r1.at[k], first_to)

    def forward_first(k):
        return remote(img.at[1, rows(k)], img.at[2, rows(k)], sf.at[k], r2.at[k], across)

    def forward_main(k):
        return remote(img.at[main, rows(k)], img.at[main, rows(k)], s3.at[k], r3.at[k], sibling)

    def send_part(k):
        return remote(grad.at[other, rows(k)], part.at[rows(k)], sp.at[k], rp.at[k], sibling)

    def send_first_back(k):
        return remote(grad.at[1, rows(k)], ret_far.at[rows(k)], sx.at[k], rx.at[k], first_back)

    to_across = jnp.where(b0, 1, 0)
    back = tuple(jnp.where(b0, x, y) for x, y in zip(across, up, strict=True))

    def send_main_back(k):
        return remote(
            grad.at[main, rows(k)], ret.at[to_across, rows(k)], sr.at[k], rr.at[to_across, k], back
        )

    def get_back(which, k):
        return remote(grad.at[main, rows(k)], ret.at[which, rows(k)], sr.at[k], rr.at[which, k], back)

    def send_text(k):
        return remote(
            text_grad.at[rows(q * chunks + k)], text_ret.at[rows(k)], st.at[k], rt.at[k], partner
        )

    load_own = pltpu.make_async_copy(pic, img.at[0], load_sem.at[0])
    load_text = pltpu.make_async_copy(cap, text, load_sem.at[1])
    load_text.start()
    load_own.start()

    barrier = pltpu.get_barrier_semaphore()
    for device in (sibling, down, up, across, far, partner):
        pl.semaphore_signal(barrier, inc=1, device_id=device, device_id_type=MESH)
    pl.semaphore_wait(barrier, 6)

    @pl.loop(0, chunks)
    def _(k):
        send_first(k).start()

        @pl.when(jnp.logical_not(a0))
        def _():
            send_main(k).start()

    scale, bias = scale_ref[0], bias_ref[0]
    load_text.wait()
    high, lower = halves(text[...])
    t_high[...] = high
    t_low[...] = lower
    tt_high[...] = high.T
    tt_low[...] = lower.T
    text_grad[...] = jnp.zeros_like(text_grad)
    load_own.wait()

    def score(slot, k, size, own):
        i_high, i_low = halves(img[slot, rows(k, size)])
        both = dot(jnp.concatenate([i_high, i_low], 0), tt_high[...])
        logits = scale * (both[:size] + both[size:] + dot(i_high, tt_low[...])) + bias
        if own:
            row = lax.broadcasted_iota(jnp.int32, logits.shape, 0) + (p * half + k * size)
            sign = jnp.where(row == lax.broadcasted_iota(jnp.int32, logits.shape, 1), -1.0, 1.0)
            coef = sign * jax.nn.sigmoid(sign * logits)
        else:
            coef = jax.nn.sigmoid(logits)
        c_high, c_low = halves(scale * coef)
        both = dot(jnp.concatenate([c_high, c_low], 0), t_high[...])
        grad[slot, rows(k, size)] = both[:size] + both[size:] + dot(c_high, t_low[...])
        text_grad[...] += lax.dot_general(
            jnp.concatenate([c_high, c_low, c_high], 0),
            jnp.concatenate([i_high, i_high, i_low], 0),
            (((0,), (0,)), ((), ())),
            preferred_element_type=F32,
        )

    @pl.loop(0, half // OWN_CHUNK)
    def _(k):
        score(0, k, OWN_CHUNK, True)

    @pl.loop(0, chunks)
    def _(k):
        send_first(k).wait_recv()

        @pl.when(a1)
        def _():
            forward_first(k).start()

        score(1, k, CHUNK, False)

        @pl.when(jnp.logical_not(a1))
        def _():
            send_first_back(k).start()

        send_main(k).wait_recv()
        forward_main(k).start()
        score(main, k, CHUNK, False)
        forward_main(k).wait_recv()
        score(other, k, CHUNK, False)
        send_part(k).start()

    @pl.loop(0, chunks)
    def _(k):
        send_text(k).start()
        send_part(k).wait_recv()
        grad[main, rows(k)] += part[rows(k)]
        send_main_back(k).start()

    @pl.loop(0, chunks)
    def _(k):
        @pl.when(a1)
        def _():
            get_back(1, k).wait_recv()
            grad[1, rows(k)] += ret[1, rows(k)]
            send_first_back(k).start()

        @pl.when(jnp.logical_not(a0))
        def _():
            get_back(0, k).wait_recv()
            grad[0, rows(k)] += ret[0, rows(k)]

        send_text(k).wait_recv()
        text_grad[rows(p * chunks + k)] += text_ret[rows(k)]
        pltpu.make_async_copy(
            text_grad.at[rows(p * chunks + k)], text_out.at[rows(k)], out_sem.at[0, k]
        ).start()
        send_first_back(k).wait_recv()
        grad[0, rows(k)] += ret_far[rows(k)]
        pltpu.make_async_copy(grad.at[0, rows(k)], image_out.at[rows(k)], out_sem.at[1, k]).start()

    @pl.loop(0, chunks)
    def _(k):
        send_first(k).wait_send()

        @pl.when(jnp.logical_not(a0))
        def _():
            send_main(k).wait_send()

        @pl.when(a1)
        def _():
            forward_first(k).wait_send()

        forward_main(k).wait_send()
        send_part(k).wait_send()
        send_main_back(k).wait_send()
        send_first_back(k).wait_send()
        send_text(k).wait_send()
        pltpu.make_async_copy(
            text_grad.at[rows(p * chunks + k)], text_out.at[rows(k)], out_sem.at[0, k]
        ).wait()
        pltpu.make_async_copy(grad.at[0, rows(k)], image_out.at[rows(k)], out_sem.at[1, k]).wait()


def solution(mesh):
    n = mesh.shape["dp"]

    def shards(picture_features, caption_features, sharpness_factor, score_intercept):
        half, width = picture_features.shape
        words = caption_features.shape[0]
        chunks = half // CHUNK
        dma = pltpu.SemaphoreType.DMA
        return pl.pallas_call(
            functools.partial(kernel, n),
            name="window_grads",
            out_shape=[jax.ShapeDtypeStruct((half, width), F32)] * 2,
            in_specs=[pl.BlockSpec(memory_space=pltpu.SMEM)] * 2 + [pl.BlockSpec(memory_space=pl.ANY)] * 2,
            out_specs=[pl.BlockSpec(memory_space=pl.ANY)] * 2,
            scratch_shapes=[
                pltpu.VMEM((4, half, width), F32),
                pltpu.VMEM((words, width), F32),
                pltpu.VMEM((words, width), BF16),
                pltpu.VMEM((words, width), BF16),
                pltpu.VMEM((width, words), BF16),
                pltpu.VMEM((width, words), BF16),
                pltpu.VMEM((4, half, width), F32),
                pltpu.VMEM((words, width), F32),
                pltpu.VMEM((half, width), F32),
                pltpu.VMEM((2, half, width), F32),
                pltpu.VMEM((half, width), F32),
                pltpu.VMEM((half, width), F32),
                dma((2,)),
                dma((2, chunks)),
            ]
            + [dma((chunks,))] * 12
            + [dma((2, chunks)), dma((chunks,)), dma((chunks,))],
            compiler_params=pltpu.CompilerParams(
                collective_id=0, has_side_effects=True, vmem_limit_bytes=48 * 2**20
            ),
            cost_estimate=pl.CostEstimate(
                flops=4 * 3 * 2 * half * words * width, bytes_accessed=4 * width * (3 * half + words), transcendentals=0
            ),
        )(sharpness_factor, score_intercept, picture_features, caption_features)

    return jax.shard_map(
        shards,
        mesh=mesh,
        in_specs=(P(("dp", "pair"), None), P("dp", None), P(), P()),
        out_specs=(P(("dp", "pair"), None), P(("dp", "pair"), None)),
        check_vma=False,
    )
```

time: 280 us -> 90.8 us (0.32)
  the two profiles are of different devices: /device:TPU:1 before, /device:TPU:6 now
where the time goes in v1:
time: 90.8 us; the launch traced here: 90.5 us
  Pallas kernels  83.7 us (92%)
  local copies, waits for them, and re-layouts  4.96 us (5%)
  between operations  1.94 us (2%)
    pallas_call x1, Pallas kernels, shards(): pl.pallas_call(functools.partial(kernel, n), name='window_grads', out_sha...  83.7 us
    unnamed x6, local copies, waits for them, and re-layouts  4.96 us

profile of v1, /device:TPU:6, one launch (start us, length us, event | category | flops | bytes accessed | tf_op | source)
XLA Modules:
  0.0 90.5 jit_solution(1334217645607419090)
XLA Ops:
  1.9 0.0 copy-start
  1.9 1.7 %copy-done = f32[512,1152]{1,0:T(8,128)S(1)} copy-done((f32[512,1152]{1,0:T(8,128)S(1)}, f32[512,1152]{1,0:T(8,128)}, u32[]{:S(2)}) %copy-start) | copy-done | bytes 2359320
  3.6 0.0 copy-start.1
  3.6 1.3 %copy-done.1 = f32[256,1152]{1,0:T(8,128)S(1)} copy-done((f32[256,1152]{1,0:T(8,128)S(1)}, f32[256,1152]{1,0:T(8,128)}, u32[]{:S(2)}) %copy-start.1) | copy-done | bytes 1179672
  4.9 83.7 %window_grads.1 = (f32[256,1152]{1,0:T(8,128)S(1)}, f32[256,1152]{1,0:T(8,128)S(1)}) custom-call(f32[1]{0:T(128)S(6)} %copy.8.scale_ref, f32[1]{0:T(128)S(6)} %copy.9.bias_ref, f32[256,1152]{1,0:T(8,128)S(1)} %copy-done.1, f32[512,1152]{1,0:T(8,128)S(1)} %copy-done), custom_call_target="tpu_custom_call" | custom-call | flops 3623878656 | bytes 5898240 | tf_op jit(solution)/shard_map/window_grads/pallas_call | solution.py:235
  88.5 1.0 %copy.10 = f32[256,1152]{1,0:T(8,128)} copy(f32[256,1152]{1,0:T(8,128)S(1)} %get-tuple-element.4) | data formatting | bytes 2359296
  89.5 1.0 %copy.11 = f32[256,1152]{1,0:T(8,128)} copy(f32[256,1152]{1,0:T(8,128)S(1)} %get-tuple-element.5) | data formatting | bytes 2359296
Async XLA Ops:
  1.9 1.7 %copy-start = (f32[512,1152]{1,0:T(8,128)S(1)}, f32[512,1152]{1,0:T(8,128)}, u32[]{:S(2)}) copy-start(f32[512,1152]{1,0:T(8,128)} %cap.1) | copy-start | bytes 7077892
  3.6 1.3 %copy-start.1 = (f32[256,1152]{1,0:T(8,128)S(1)}, f32[256,1152]{1,0:T(8,128)}, u32[]{:S(2)}) copy-start(f32[256,1152]{1,0:T(8,128)} %pic.1) | copy-start | bytes 3538948

commit v2 on v1

--- a/solution.py
+++ b/solution.py
@@ -10,7 +10,6 @@
 MESH = pl.DeviceIdType.MESH
 F32, BF16 = jnp.float32, jnp.bfloat16
 CHUNK = 64
-OWN_CHUNK = 128
 
 
 def halves(value):
@@ -25,8 +24,8 @@
 def kernel(
     n, scale_ref, bias_ref, pic, cap, image_out, text_out,
     img, text, t_high, t_low, tt_high, tt_low, grad, text_grad,
-    part, ret, ret_far, text_ret,
-    load_sem, out_sem, s1, s2, s3, sf, sp, sr, sx, st, r1, r2, r3, rp, rr, rx, rt,
+    part, ret, ret_far, text_ret, stage, stage_back,
+    load_sem, out_sem, s1, s2, s3, sf, sp, sr, sx, st, sg, sb, r1, r2, r3, rp, rg, rb, rr, rx, rt, ready,
 ):
     dp, p = lax.axis_index("dp"), lax.axis_index("pair")
     half, words = pic.shape[0], cap.shape[0]
@@ -36,6 +35,7 @@
     a0 = low & (core == 0)
     a1 = low & (core == 1)
     b0 = jnp.logical_not(low) & (core == 0)
+    b1 = jnp.logical_not(low) & (core == 1)
 
     def there(step, row):
         return (lax.rem(dp + step + n, n), row)
@@ -49,6 +49,7 @@
     first_back = there(jnp.where(core == 1, 3, 1), p)
     partner = (dp, q)
     main, other = 2 + core, 3 - core
+    next_up, next_down = there(4, p), there(-4, p)
 
     def rows(k, size=CHUNK):
         return pl.ds(pl.multiple_of(k * size, size), size)
@@ -72,7 +73,16 @@
         return remote(pic.at[rows(k)], img.at[1, rows(k)], s1.at[k], r1.at[k], first_to)
 
     def forward_first(k):
-        return remote(img.at[1, rows(k)], img.at[2, rows(k)], sf.at[k], r2.at[k], across)
+        return remote(img.at[1, rows(k)], img.at[other, rows(k)], sf.at[k], r2.at[k], across)
+
+    def send_stage(k):
+        return remote(pic.at[rows(k)], stage.at[rows(k)], s2.at[k], rg.at[k], up)
+
+    def send_far(k):
+        return remote(pic.at[rows(k)], img.at[3, rows(k)], s2.at[k], r2.at[k], down)
+
+    def forward_stage(k):
+        return remote(stage.at[rows(k)], img.at[3, rows(k)], sg.at[k], r2.at[k], next_down)
 
     def forward_main(k):
         return remote(img.at[main, rows(k)], img.at[main, rows(k)], s3.at[k], r3.at[k], sibling)
@@ -91,6 +101,12 @@
             grad.at[main, rows(k)], ret.at[to_across, rows(k)], sr.at[k], rr.at[to_across, k], back
         )
 
+    def send_stage_back(k):
+        return remote(grad.at[main, rows(k)], stage_back.at[rows(k)], sr.at[k], rb.at[k], next_up)
+
+    def forward_stage_back(k):
+        return remote(stage_back.at[rows(k)], ret.at[0, rows(k)], sb.at[k], rr.at[0, k], down)
+
     def get_back(which, k):
         return remote(grad.at[main, rows(k)], ret.at[which, rows(k)], sr.at[k], rr.at[which, k], back)
 
@@ -104,18 +120,59 @@
     load_text.start()
     load_own.start()
 
+    below = tuple(
+        jnp.where(core == 0, x, jnp.where(low, y, z)) for x, y, z in zip(far, down, next_down, strict=True)
+    )
     barrier = pltpu.get_barrier_semaphore()
-    for device in (sibling, down, up, across, far, partner):
-        pl.semaphore_signal(barrier, inc=1, device_id=device, device_id_type=MESH)
-    pl.semaphore_wait(barrier, 6)
+
+    def greet(device, semaphore=barrier):
+        pl.semaphore_signal(semaphore, inc=1, device_id=device, device_id_type=MESH)
+
+    greet(below)
+    greet(sibling)
+    greet(partner)
+
+    @pl.when(low)
+    def _():
+        greet(up)
+
+    @pl.when(jnp.logical_not(low))
+    def _():
+        greet(down)
+
+    @pl.when(a1 | b0)
+    def _():
+        greet(across)
+
+    pl.semaphore_wait(barrier, jnp.where(a0, 3, jnp.where(b0, 4, jnp.where(a1, 5, 6))))
+
+    @pl.when(core == 1)
+    def _():
+        greet(far, ready)
+
+    @pl.when(b1)
+    def _():
+        greet(up, ready)
+        greet(next_up, ready)
 
     @pl.loop(0, chunks)
     def _(k):
-        send_first(k).start()
-
-        @pl.when(jnp.logical_not(a0))
+        @pl.when(b0)
         def _():
             send_main(k).start()
+
+        @pl.when(a1 & (k < 2))
+        def _():
+            send_stage(k).start()
+
+        @pl.when(core == 1)
+        def _():
+            send_first(k).start()
+
+    @pl.when(core == 0)
+    def _():
+        pl.semaphore_wait(ready, 1)
+        each(lambda k: send_first(k).start())
 
     scale, bias = scale_ref[0], bias_ref[0]
     load_text.wait()
@@ -127,16 +184,13 @@
     text_grad[...] = jnp.zeros_like(text_grad)
     load_own.wait()
 
-    def score(slot, k, size, own):
+    def score(slot, k, size):
         i_high, i_low = halves(img[slot, rows(k, size)])
         both = dot(jnp.concatenate([i_high, i_low], 0), tt_high[...])
         logits = scale * (both[:size] + both[size:] + dot(i_high, tt_low[...])) + bias
-        if own:
-            row = lax.broadcasted_iota(jnp.int32, logits.shape, 0) + (p * half + k * size)
-            sign = jnp.where(row == lax.broadcasted_iota(jnp.int32, logits.shape, 1), -1.0, 1.0)
-            coef = sign * jax.nn.sigmoid(sign * logits)
-        else:
-            coef = jax.nn.sigmoid(logits)
+        row = lax.broadcasted_iota(jnp.int32, logits.shape, 0) + jnp.where(slot == 0, p * half + k * size, words)
+        sign = jnp.where(row == lax.broadcasted_iota(jnp.int32, logits.shape, 1), -1.0, 1.0)
+        coef = sign * jax.nn.sigmoid(sign * logits)
         c_high, c_low = halves(scale * coef)
         both = dot(jnp.concatenate([c_high, c_low], 0), t_high[...])
         grad[slot, rows(k, size)] = both[:size] + both[size:] + dot(c_high, t_low[...])
@@ -147,46 +201,131 @@
             preferred_element_type=F32,
         )
 
-    @pl.loop(0, half // OWN_CHUNK)
-    def _(k):
-        score(0, k, OWN_CHUNK, True)
-
-    @pl.loop(0, chunks)
-    def _(k):
-        send_first(k).wait_recv()
-
-        @pl.when(a1)
+    def pass_on(k):
+        @pl.when(a1 | b0)
+        def _():
+            send_first(k).wait_recv()
+
+        @pl.when(a1 | (b0 & (k < 2)))
         def _():
             forward_first(k).start()
 
-        score(1, k, CHUNK, False)
-
-        @pl.when(jnp.logical_not(a1))
-        def _():
-            send_first_back(k).start()
-
-        send_main(k).wait_recv()
-        forward_main(k).start()
-        score(main, k, CHUNK, False)
-        forward_main(k).wait_recv()
-        score(other, k, CHUNK, False)
-        send_part(k).start()
-
-    @pl.loop(0, chunks)
-    def _(k):
-        send_text(k).start()
+        @pl.when((b1 & (k == 0)) | (a1 & (k == 3)))
+        def _():
+            pl.semaphore_wait(ready, 1)
+
+        @pl.when(b1 & (k < 2))
+        def _():
+            send_stage(k).wait_recv()
+            forward_stage(k).start()
+
+        @pl.when((core == 1) & (k == 3))
+        def _():
+            for u in (2, 3):
+                send_far(u).start()
+
+    def arrives(slot, k):
+        @pl.when((slot == 1) & (a0 | b1))
+        def _():
+            send_first(k).wait_recv()
+
+        @pl.when(slot == main)
+        def _():
+            send_main(k).wait_recv()
+            forward_main(k).start()
+
+        @pl.when(slot == other)
+        def _():
+            forward_main(k).wait_recv()
+
+    def done(slot, k, count):
+        @pl.when(slot == other)
+        def _():
+            for u in range(count):
+                send_part(k + u).start()
+
+    @pl.loop(0, 6)
+    def _(j):
+        slot = jnp.where(j < 4, j // 2 + j // 3, jnp.where(j == 5, 1, jnp.where(low, 2, 3)))
+        part_at = jnp.where((j == 1) | (j == 5) | ((j == 4) & low), 1, 0)
+
+        @pl.when((j > 0) & (j < 5))
+        def _():
+            pass_on(j - 1)
+
+        for u in range(2):
+            arrives(slot, 2 * part_at + u)
+        score(slot, part_at, 2 * CHUNK)
+        done(slot, 2 * part_at, 2)
+
+        @pl.when((slot == 1) & ((core == 0) | (b1 & (j == 2))))
+        def _():
+            for u in range(2):
+                send_first_back(2 * part_at + u).start()
+
+    def give_back(k):
         send_part(k).wait_recv()
         grad[main, rows(k)] += part[rows(k)]
-        send_main_back(k).start()
+
+        @pl.when(b1)
+        def _():
+            send_stage_back(k).start()
+
+        @pl.when(jnp.logical_not(b1))
+        def _():
+            send_main_back(k).start()
+
+    def give_back_two(first):
+        for u in range(2):
+            give_back(first + u)
+
+    @pl.when(jnp.logical_not(low))
+    def _():
+        give_back_two(0)
 
     @pl.loop(0, chunks)
-    def _(k):
-        @pl.when(a1)
-        def _():
+    def _(j):
+        slot = jnp.where(low, 3, 2 + lax.rem(j, 2))
+        k = jnp.where(low, j, 2 + j // 2)
+        arrives(slot, k)
+        score(slot, k, CHUNK)
+        done(slot, k, 1)
+
+        @pl.when(low & (j == 2))
+        def _():
+            give_back_two(0)
+
+        @pl.when(a0 & (j == 2))
+        def _():
+            give_back_two(2)
+
+    each(lambda k: send_text(k).start())
+
+    @pl.when(jnp.logical_not(a0))
+    def _():
+        give_back_two(2)
+
+    @pl.when(b1)
+    def _():
+        def step(k):
+            send_stage_back(k).wait_recv()
+            forward_stage_back(k).start()
+
+        for u in (2, 3):
+            send_first_back(u).start()
+        each(step)
+
+    @pl.when(a1)
+    def _():
+        def chain(k):
             get_back(1, k).wait_recv()
             grad[1, rows(k)] += ret[1, rows(k)]
             send_first_back(k).start()
 
+        each(chain)
+
+    @pl.loop(0, chunks)
+    def _(k):
         @pl.when(jnp.logical_not(a0))
         def _():
             get_back(0, k).wait_recv()
@@ -205,11 +344,23 @@
     def _(k):
         send_first(k).wait_send()
 
-        @pl.when(jnp.logical_not(a0))
+        @pl.when(b0)
         def _():
             send_main(k).wait_send()
 
-        @pl.when(a1)
+        @pl.when(a1 | (b1 & (k > 1)))
+        def _():
+            send_stage(k).wait_send()
+
+        @pl.when(b1 & (k < 2))
+        def _():
+            forward_stage(k).wait_send()
+
+        @pl.when(b1)
+        def _():
+            forward_stage_back(k).wait_send()
+
+        @pl.when(a1 | (b0 & (k < 2)))
         def _():
             forward_first(k).wait_send()
 
@@ -251,13 +402,15 @@
                 pltpu.VMEM((2, half, width), F32),
                 pltpu.VMEM((half, width), F32),
                 pltpu.VMEM((half, width), F32),
+                pltpu.VMEM((half, width), F32),
+                pltpu.VMEM((half, width), F32),
                 dma((2,)),
                 dma((2, chunks)),
             ]
-            + [dma((chunks,))] * 12
-            + [dma((2, chunks)), dma((chunks,)), dma((chunks,))],
+            + [dma((chunks,))] * 16
+            + [dma((2, chunks)), dma((chunks,)), dma((chunks,)), pltpu.SemaphoreType.REGULAR],
             compiler_params=pltpu.CompilerParams(
-                collective_id=0, has_side_effects=True, vmem_limit_bytes=48 * 2**20
+                collective_id=0, has_side_effects=True, vmem_limit_bytes=62 * 2**20
             ),
             cost_estimate=pl.CostEstimate(
                 flops=4 * 3 * 2 * half * words * width, bytes_accessed=4 * width * (3 * half + words), transcendentals=0

time: 90.8 us -> 81.5 us (0.90)
  the two profiles are of different devices: /device:TPU:6 before, /device:TPU:8 now
where the time goes in v2:
time: 81.5 us; the launch traced here: 81.4 us
  Pallas kernels  76 us (93%)
  local copies, waits for them, and re-layouts  3.47 us (4%)
  between operations  1.94 us (2%)
    pallas_call x1, Pallas kernels, shards(): pl.pallas_call(functools.partial(kernel, n), name='window_grads', out_sha...  76 us
    unnamed x4, local copies, waits for them, and re-layouts  3.47 us

profile of v2, /device:TPU:8, one launch (start us, length us, event | category | flops | bytes accessed | tf_op | source)
XLA Modules:
  0.0 81.4 jit_solution(10792725570011352757)
XLA Ops:
  1.9 76.0 %window_grads.1 = (f32[256,1152]{1,0:T(8,128)}, f32[256,1152]{1,0:T(8,128)}) custom-call(f32[1]{0:T(128)S(6)} %copy.8.scale_ref, f32[1]{0:T(128)S(6)} %copy.9.bias_ref, f32[256,1152]{1,0:T(8,128)} %pic.1, f32[512,1152]{1,0:T(8,128)} %cap.1), custom_call_target="tpu_custom_call" | custom-call | flops 3623878656 | bytes 5898240 | tf_op jit(solution)/shard_map/window_grads/pallas_call | solution.py:386
  77.9 0.0 copy-start
  77.9 2.5 %copy.10 = f32[256,1152]{1,0:T(8,128)} copy(f32[256,1152]{1,0:T(8,128)} %get-tuple-element.4) | data formatting | bytes 2359296
  80.3 0.0 copy-done
  80.4 1.0 %copy.11 = f32[256,1152]{1,0:T(8,128)} copy(f32[256,1152]{1,0:T(8,128)S(1)} %copy-done) | data formatting | bytes 2359296
Async XLA Ops:
  77.9 2.5 %copy-start = (f32[256,1152]{1,0:T(8,128)S(1)}, f32[256,1152]{1,0:T(8,128)}, u32[]{:S(2)}) copy-start(f32[256,1152]{1,0:T(8,128)} %get-tuple-element.5) | copy-start | bytes 3538948

commit v3 on v2

--- a/solution.py
+++ b/solution.py
@@ -25,7 +25,7 @@
     n, scale_ref, bias_ref, pic, cap, image_out, text_out,
     img, text, t_high, t_low, tt_high, tt_low, grad, text_grad,
     part, ret, ret_far, text_ret, stage, stage_back,
-    load_sem, out_sem, s1, s2, s3, sf, sp, sr, sx, st, sg, sb, r1, r2, r3, rp, rg, rb, rr, rx, rt, ready,
+    load_sem, out_sem, s1, s2, s3, sf, sp, sr, sx, st, sg, sb, r1, r2, r3, rp, rg, rb, rr, rx, rt, ready, clear,
 ):
     dp, p = lax.axis_index("dp"), lax.axis_index("pair")
     half, words = pic.shape[0], cap.shape[0]
@@ -246,8 +246,10 @@
 
     @pl.loop(0, 6)
     def _(j):
-        slot = jnp.where(j < 4, j // 2 + j // 3, jnp.where(j == 5, 1, jnp.where(low, 2, 3)))
-        part_at = jnp.where((j == 1) | (j == 5) | ((j == 4) & low), 1, 0)
+        fifth = jnp.where(low, 2, jnp.where(core == 0, 1, 3))
+        sixth = jnp.where(b0, 3, 1)
+        slot = jnp.where(j < 4, j // 2 + j // 3, jnp.where(j == 4, fifth, sixth))
+        part_at = jnp.where((j == 1) | ((j > 3) & (slot != 3)), 1, 0)
 
         @pl.when((j > 0) & (j < 5))
         def _():
@@ -275,23 +277,47 @@
         def _():
             send_main_back(k).start()
 
+    def stage_back_arrives(k):
+        send_stage_back(k).wait_recv()
+        forward_stage_back(k).start()
+
     def give_back_two(first):
         for u in range(2):
             give_back(first + u)
 
-    @pl.when(jnp.logical_not(low))
+    @pl.when(b0)
     def _():
         give_back_two(0)
+
+    def main_arrives(k):
+        send_main(k).wait_recv()
+        forward_main(k).start()
 
     @pl.loop(0, chunks)
     def _(j):
-        slot = jnp.where(low, 3, 2 + lax.rem(j, 2))
+        slot = jnp.where(low, 3, jnp.where(lax.rem(j, 2) == 0, main, other))
         k = jnp.where(low, j, 2 + j // 2)
-        arrives(slot, k)
+
+        @pl.when(low)
+        def _():
+            arrives(slot, k)
+
+        @pl.when(jnp.logical_not(low) & (j < 2))
+        def _():
+            main_arrives(2 + j)
+
+        @pl.when(jnp.logical_not(low) & (slot == other))
+        def _():
+            forward_main(k).wait_recv()
+
         score(slot, k, CHUNK)
         done(slot, k, 1)
 
-        @pl.when(low & (j == 2))
+        @pl.when(b1 & (j == 2))
+        def _():
+            stage_back_arrives(0)
+
+        @pl.when((low & (j == 2)) | (b1 & (j == 0)))
         def _():
             give_back_two(0)
 
@@ -305,15 +331,19 @@
     def _():
         give_back_two(2)
 
+    @pl.when(b0)
+    def _():
+        for u in (2, 3):
+            send_main_back(u).wait_send()
+        pl.semaphore_signal(clear, inc=1, device_id=sibling, device_id_type=MESH)
+
     @pl.when(b1)
     def _():
-        def step(k):
-            send_stage_back(k).wait_recv()
-            forward_stage_back(k).start()
-
         for u in (2, 3):
             send_first_back(u).start()
-        each(step)
+        pl.semaphore_wait(clear, 1)
+        for u in (1, 2, 3):
+            stage_back_arrives(u)
 
     @pl.when(a1)
     def _():
@@ -366,7 +396,11 @@
 
         forward_main(k).wait_send()
         send_part(k).wait_send()
-        send_main_back(k).wait_send()
+
+        @pl.when(jnp.logical_not(b0 & (k > 1)))
+        def _():
+            send_main_back(k).wait_send()
+
         send_first_back(k).wait_send()
         send_text(k).wait_send()
         pltpu.make_async_copy(
@@ -408,7 +442,7 @@
                 dma((2, chunks)),
             ]
             + [dma((chunks,))] * 16
-            + [dma((2, chunks)), dma((chunks,)), dma((chunks,)), pltpu.SemaphoreType.REGULAR],
+            + [dma((2, chunks)), dma((chunks,)), dma((chunks,)), pltpu.SemaphoreType.REGULAR, pltpu.SemaphoreType.REGULAR],
             compiler_params=pltpu.CompilerParams(
                 collective_id=0, has_side_effects=True, vmem_limit_bytes=62 * 2**20
             ),

time: 81.5 us -> 74.8 us (0.918)
  the two profiles are of different devices: /device:TPU:8 before, /device:TPU:1 now
where the time goes in v3:
time: 74.8 us; the launch traced here: 74.6 us
  Pallas kernels  69.2 us (93%)
  local copies, waits for them, and re-layouts  3.47 us (5%)
  between operations  1.94 us (3%)
    pallas_call x1, Pallas kernels, shards(): pl.pallas_call(functools.partial(kernel, n), name='window_grads', out_sha...  69.2 us
    unnamed x4, local copies, waits for them, and re-layouts  3.47 us

profile of v3, /device:TPU:1, one launch (start us, length us, event | category | flops | bytes accessed | tf_op | source)
XLA Modules:
  0.0 74.6 jit_solution(7410762528931322512)
XLA Ops:
  1.9 69.2 %window_grads.1 = (f32[256,1152]{1,0:T(8,128)}, f32[256,1152]{1,0:T(8,128)}) custom-call(f32[1]{0:T(128)S(6)} %copy.8.scale_ref, f32[1]{0:T(128)S(6)} %copy.9.bias_ref, f32[256,1152]{1,0:T(8,128)} %pic.1, f32[512,1152]{1,0:T(8,128)} %cap.1), custom_call_target="tpu_custom_call" | custom-call | flops 3623878656 | bytes 5898240 | tf_op jit(solution)/shard_map/window_grads/pallas_call | solution.py:420
  71.1 0.0 copy-start
  71.2 2.5 %copy.10 = f32[256,1152]{1,0:T(8,128)} copy(f32[256,1152]{1,0:T(8,128)} %get-tuple-element.4) | data formatting | bytes 2359296
  73.6 0.0 copy-done
  73.6 1.0 %copy.11 = f32[256,1152]{1,0:T(8,128)} copy(f32[256,1152]{1,0:T(8,128)S(1)} %copy-done) | data formatting | bytes 2359296
Async XLA Ops:
  71.1 2.5 %copy-start = (f32[256,1152]{1,0:T(8,128)S(1)}, f32[256,1152]{1,0:T(8,128)}, u32[]{:S(2)}) copy-start(f32[256,1152]{1,0:T(8,128)} %get-tuple-element.5) | copy-start | bytes 3538948

commit v4 on v3

--- a/solution.py
+++ b/solution.py
@@ -10,6 +10,7 @@
 MESH = pl.DeviceIdType.MESH
 F32, BF16 = jnp.float32, jnp.bfloat16
 CHUNK = 64
+DEPTH = 16
 
 
 def halves(value):
@@ -36,6 +37,7 @@
     a1 = low & (core == 1)
     b0 = jnp.logical_not(low) & (core == 0)
     b1 = jnp.logical_not(low) & (core == 1)
+    edge = lax.rem(dp // 4, DEPTH) == 0
 
     def there(step, row):
         return (lax.rem(dp + step + n, n), row)
@@ -169,10 +171,11 @@
         def _():
             send_first(k).start()
 
-    @pl.when(core == 0)
-    def _():
+    def send_below():
         pl.semaphore_wait(ready, 1)
         each(lambda k: send_first(k).start())
+
+    pl.when((core == 0) & jnp.logical_not(edge))(send_below)
 
     scale, bias = scale_ref[0], bias_ref[0]
     load_text.wait()
@@ -201,6 +204,14 @@
             preferred_element_type=F32,
         )
 
+    def send_last_two():
+        @pl.when(a1)
+        def _():
+            pl.semaphore_wait(ready, 1)
+
+        for u in (2, 3):
+            send_far(u).start()
+
     def pass_on(k):
         @pl.when(a1 | b0)
         def _():
@@ -210,7 +221,7 @@
         def _():
             forward_first(k).start()
 
-        @pl.when((b1 & (k == 0)) | (a1 & (k == 3)))
+        @pl.when(b1 & (k == 0))
         def _():
             pl.semaphore_wait(ready, 1)
 
@@ -219,10 +230,7 @@
             send_stage(k).wait_recv()
             forward_stage(k).start()
 
-        @pl.when((core == 1) & (k == 3))
-        def _():
-            for u in (2, 3):
-                send_far(u).start()
+        pl.when((k == 3) & (b1 | (a1 & jnp.logical_not(edge))))(send_last_two)
 
     def arrives(slot, k):
         @pl.when((slot == 1) & (a0 | b1))
@@ -259,6 +267,8 @@
             arrives(slot, 2 * part_at + u)
         score(slot, part_at, 2 * CHUNK)
         done(slot, 2 * part_at, 2)
+        pl.when((core == 0) & edge & (j == 2))(send_below)
+        pl.when(a1 & edge & (j == 5))(send_last_two)
 
         @pl.when((slot == 1) & ((core == 0) | (b1 & (j == 2))))
         def _():
@@ -302,9 +312,13 @@
         def _():
             arrives(slot, k)
 
-        @pl.when(jnp.logical_not(low) & (j < 2))
-        def _():
-            main_arrives(2 + j)
+        @pl.when(jnp.logical_not(low) & (j == 0))
+        def _():
+            main_arrives(2)
+
+        @pl.when((b1 & (j == 1)) | (b0 & (j == 2)))
+        def _():
+            main_arrives(3)
 
         @pl.when(jnp.logical_not(low) & (slot == other))
         def _():
@@ -313,7 +327,7 @@
         score(slot, k, CHUNK)
         done(slot, k, 1)
 
-        @pl.when(b1 & (j == 2))
+        @pl.when(b1 & (j == 2) & jnp.logical_not(edge))
         def _():
             stage_back_arrives(0)
 
@@ -342,6 +356,11 @@
         for u in (2, 3):
             send_first_back(u).start()
         pl.semaphore_wait(clear, 1)
+
+        @pl.when(edge)
+        def _():
+            stage_back_arrives(0)
+
         for u in (1, 2, 3):
             stage_back_arrives(u)
 
@@ -444,7 +463,7 @@
             + [dma((chunks,))] * 16
             + [dma((2, chunks)), dma((chunks,)), dma((chunks,)), pltpu.SemaphoreType.REGULAR, pltpu.SemaphoreType.REGULAR],
             compiler_params=pltpu.CompilerParams(
-                collective_id=0, has_side_effects=True, vmem_limit_bytes=62 * 2**20
+                collective_id=0, has_side_effects=True, vmem_limit_bytes=51 * 2**20
             ),
             cost_estimate=pl.CostEstimate(
                 flops=4 * 3 * 2 * half * words * width, bytes_accessed=4 * width * (3 * half + words), transcendentals=0

time: 74.8 us -> 72.6 us (0.971)
  the two profiles are of different devices: /device:TPU:1 before, /device:TPU:8 now
where the time goes in v4:
time: 72.6 us; the launch traced here: 72.5 us
  Pallas kernels  68.5 us (94%)
  local copies, waits for them, and re-layouts  2.03 us (3%)
  between operations  1.93 us (3%)
    pallas_call x1, Pallas kernels, shards(): pl.pallas_call(functools.partial(kernel, n), name='window_grads', out_sha...  68.5 us
    unnamed x2, local copies, waits for them, and re-layouts  2.03 us

profile of v4, /device:TPU:8, one launch (start us, length us, event | category | flops | bytes accessed | tf_op | source)
XLA Modules:
  0.0 72.5 jit_solution(7578808759181474513)
XLA Ops:
  1.9 68.5 %window_grads.1 = (f32[256,1152]{1,0:T(8,128)S(1)}, f32[256,1152]{1,0:T(8,128)S(1)}) custom-call(f32[1]{0:T(128)S(6)} %copy.8.scale_ref, f32[1]{0:T(128)S(6)} %copy.9.bias_ref, f32[256,1152]{1,0:T(8,128)} %pic.1, f32[512,1152]{1,0:T(8,128)} %cap.1), custom_call_target="tpu_custom_call" | custom-call | flops 3623878656 | bytes 5898240 | tf_op jit(solution)/shard_map/window_grads/pallas_call | solution.py:439
  70.4 1.0 %copy.10 = f32[256,1152]{1,0:T(8,128)} copy(f32[256,1152]{1,0:T(8,128)S(1)} %get-tuple-element.4) | data formatting | bytes 2359296
  71.5 1.0 %copy.11 = f32[256,1152]{1,0:T(8,128)} copy(f32[256,1152]{1,0:T(8,128)S(1)} %get-tuple-element.5) | data formatting | bytes 2359296

commit v5 on v4

--- a/solution.py
+++ b/solution.py
@@ -205,10 +205,7 @@
         )
 
     def send_last_two():
-        @pl.when(a1)
-        def _():
-            pl.semaphore_wait(ready, 1)
-
+        pl.semaphore_wait(ready, 1)
         for u in (2, 3):
             send_far(u).start()
 
@@ -217,7 +214,7 @@
         def _():
             send_first(k).wait_recv()
 
-        @pl.when(a1 | (b0 & (k < 2)))
+        @pl.when(a1 | b0)
         def _():
             forward_first(k).start()
 
@@ -230,7 +227,7 @@
             send_stage(k).wait_recv()
             forward_stage(k).start()
 
-        pl.when((k == 3) & (b1 | (a1 & jnp.logical_not(edge))))(send_last_two)
+        pl.when((k == 3) & a1 & jnp.logical_not(edge))(send_last_two)
 
     def arrives(slot, k):
         @pl.when((slot == 1) & (a0 | b1))
@@ -397,7 +394,7 @@
         def _():
             send_main(k).wait_send()
 
-        @pl.when(a1 | (b1 & (k > 1)))
+        @pl.when(a1)
         def _():
             send_stage(k).wait_send()
 
@@ -409,7 +406,7 @@
         def _():
             forward_stage_back(k).wait_send()
 
-        @pl.when(a1 | (b0 & (k < 2)))
+        @pl.when(a1 | b0)
         def _():
             forward_first(k).wait_send()
 

time: 72.6 us -> 69.5 us (0.957)
  Pallas kernels: 68.5 us -> 65.4 us
    pallas_call x1, Pallas kernels: 68.5 us -> 65.4 us  [shards(): pl.pallas_call(functools.partial(kernel, n), name='window_grads', out_sha...]
where the time goes in v5:
time: 69.5 us; the launch traced here: 69.4 us
  Pallas kernels  65.4 us (94%)
  local copies, waits for them, and re-layouts  2.03 us (3%)
  between operations  1.93 us (3%)
    pallas_call x1, Pallas kernels, shards(): pl.pallas_call(functools.partial(kernel, n), name='window_grads', out_sha...  65.4 us
    unnamed x2, local copies, waits for them, and re-layouts  2.03 us

profile of v5, /device:TPU:8, one launch (start us, length us, event | category | flops | bytes accessed | tf_op | source)
XLA Modules:
  0.0 69.4 jit_solution(310713002206967735)
XLA Ops:
  1.9 65.4 %window_grads.1 = (f32[256,1152]{1,0:T(8,128)S(1)}, f32[256,1152]{1,0:T(8,128)S(1)}) custom-call(f32[1]{0:T(128)S(6)} %copy.8.scale_ref, f32[1]{0:T(128)S(6)} %copy.9.bias_ref, f32[256,1152]{1,0:T(8,128)} %pic.1, f32[512,1152]{1,0:T(8,128)} %cap.1), custom_call_target="tpu_custom_call" | custom-call | flops 3623878656 | bytes 5898240 | tf_op jit(solution)/shard_map/window_grads/pallas_call | solution.py:436
  67.3 1.0 %copy.10 = f32[256,1152]{1,0:T(8,128)} copy(f32[256,1152]{1,0:T(8,128)S(1)} %get-tuple-element.4) | data formatting | bytes 2359296
  68.3 1.0 %copy.11 = f32[256,1152]{1,0:T(8,128)} copy(f32[256,1152]{1,0:T(8,128)S(1)} %get-tuple-element.5) | data formatting | bytes 2359296
